TPU v7x, 256 devices: a whole 4x4x8 slice. The times are simulated.
256 devices in a mesh: mset: 16 (over x_hi, y, core), band: 16 (over x_lo, z).
Axes of the slice: x: 4 (x_hi: 2, x_lo: 2; x = x_hi * 2 + x_lo), y: 4, z: 8, core: 2. Of those that a mesh axis runs over, the one named last changes fastest.
Arguments:
- coeffs: bfloat16 [2, 704, 61440], P(None, 'band', 'mset'), may hold values from -6 to 6
- legendre: bfloat16 [640, 704, 2048], P('mset', None, 'band'), may hold values from -0.3125 to 0.3125
- wavenumber: int32 [640], P('mset'), may hold values from 0 to 639, as said below
- band_rows: int32 [16], P('band'), may hold values from 16 to 128, as said below
Outputs:
- fourier: bfloat16 [96, 1280, 2048], P('mset', None, 'band')
Inputs may be any that keep to these rules, and one draw needn't show every extreme that they name: All entries differ; pair q stands for wavenumbers wavenumber[q] and 1279 - wavenumber[q]. Both ends of the range occur. `band_rows`: entries 2 j and 2 j + 1 are equal (a band and its mirror image); some band holds 128.
All inputs are finite; a program needn't handle non-finite values.
Results may differ from a plain program's by a relative error of at most 0.0051.
Values may be sent and summed in bfloat16 or wider, within the bound.
A program may use at most 128 MiB of HBM per device.

v0:
```python
import jax
import jax.numpy as jnp
from jax import lax
from jax.sharding import PartitionSpec as P

TRUNC = 1279


def from_partner(value, axis, bit):
    mask = 2**bit
    pairs = [(source, source ^ mask) for source in range(lax.axis_size(axis))]
    return lax.ppermute(value, axis, pairs)


def degree_weights(wavenumber, parity, row_total):
    first_count = jnp.maximum((TRUNC - wavenumber - parity) // 2 + 1, 0)
    second_count = jnp.maximum((wavenumber - parity) // 2 + 1, 0)
    row_index = jnp.arange(row_total, dtype=jnp.int32)
    in_first = row_index[:, None] < first_count[None, :]
    in_second = jnp.logical_and(
        jnp.logical_not(in_first), row_index[:, None] < (first_count + second_count)[None, :]
    )
    return jnp.stack([in_first, in_second], axis=2).astype(jnp.bfloat16)


def accumulate(running, portion, weights, legendre, block_count, block_width):
    row_count, pair_count, field_count = portion.shape
    stacked = (portion[:, :, None, :] * weights[:, :, :, None]).reshape(
        row_count, pair_count, 2 * field_count
    )

    def one_block(block_index, block_sums):
        offset = block_index * block_width
        columns = lax.dynamic_slice_in_dim(legendre, offset, block_width, 2)
        product = jnp.einsum("rpc,prl->pcl", stacked, columns, preferred_element_type=jnp.float32)
        current = lax.dynamic_slice_in_dim(block_sums, offset, block_width, 2)
        return lax.dynamic_update_slice_in_dim(block_sums, current + product, offset, 2)

    return lax.fori_loop(0, block_count, one_block, running)


def shards(coeffs, legendre, wavenumber, band_rows):
    parity = lax.axis_index("band") % 2
    pair_count = legendre.shape[0]
    row_total = legendre.shape[1]
    lat_slots = legendre.shape[2]
    field_count = coeffs.shape[2] // pair_count
    weights = degree_weights(wavenumber, parity, row_total)
    block_width = 32
    lat_count = band_rows[0]
    block_count = (lat_count + block_width - 1) // block_width
    zeros_init = jnp.zeros((pair_count, 2 * field_count, lat_slots), jnp.float32)
    own_rows = lax.dynamic_index_in_dim(
        lax.all_gather(coeffs, "band", axis=1, tiled=True), parity, 0, keepdims=False
    )
    own_rows = own_rows.reshape(own_rows.shape[0], pair_count, field_count)
    summed = accumulate(zeros_init, own_rows, weights, legendre, block_count, block_width)
    own_part = lax.optimization_barrier(summed.astype(jnp.bfloat16))
    partner_part = from_partner(own_part, "band", 0)
    own_wide = own_part.astype(jnp.float32)
    partner_wide = partner_part.astype(jnp.float32)
    grid_values = jnp.where(parity == 0, own_wide + partner_wide, partner_wide - own_wide)
    valid_lat = jnp.arange(lat_slots, dtype=jnp.int32) < lat_count
    grid_values = jnp.where(valid_lat, grid_values, 0.0).astype(jnp.bfloat16)
    by_field = jnp.swapaxes(grid_values.reshape(2 * pair_count, field_count, lat_slots), 0, 1)
    return lax.all_to_all(by_field, "mset", split_axis=0, concat_axis=1, tiled=True)


def solution(mesh):
    in_specs = (P(None, "band", "mset"), P("mset", None, "band"), P("mset"), P("band"))
    out_specs = P("mset", None, "band")
    return jax.shard_map(shards, mesh=mesh, in_specs=in_specs, out_specs=out_specs, check_vma=False)
```

profile of v0, /device:TPU:192, one launch (start us, length us, event | category | flops | bytes accessed | tf_op | source)
XLA Modules:
  0.0 339.4 jit_solution(12263412581686721495)
XLA Ops:
  6.5 0.7 all-gather.2.cloned.1.call-update
  7.9 0.7 maximum_add_fusion
  8.6 0.1 iota_compare_fusion.1
  8.8 10.3 %copy.31 = bf16[40,704,128]{1,2,0:T(8,128)(2,1)} copy(bf16[40,704,128]{2,1,0:T(8,128)(2,1)} %param.7) | data formatting | bytes 14417920
  19.2 113.3 %all-gather.2.cloned.1.call-done = bf16[2,704,3840]{2,0,1:T(2,128)(2,1)} async-done(((bf16[2,44,3840]{2,0,1:T(2,128)(2,1)}), bf16[2,704,3840]{2,0,1:T(2,128)(2,1)}) %all-gather.2.cloned.1.call-update) | async-done | bytes 10813456 | tf_op jit(solution)/shard_map/all_gather | solution.py:54
  132.5 13.9 %constant_dynamic-slice_fusion = bf16[1,704,3840]{2,0,1:T(2,128)(2,1)} fusion(bf16[2,704,3840]{2,0,1:T(2,128)(2,1)} %all-gather.2.cloned.1.call-done, s32[]{:T(128)S(6)} %select_n.43), kind=kLoop, calls=%fused_computation.28 | loop fusion | bytes 10813444 | tf_op jit(solution)/shard_map/jit(dynamic_index_in_dim)/dynamic_slice | solution.py:53
  146.3 23.5 %copy.36 = bf16[1,704,3840]{1,2,0:T(8,128)(2,1)} copy(bf16[1,704,3840]{2,0,1:T(2,128)(2,1)} %constant_dynamic-slice_fusion) | data formatting | bytes 10813440
  169.9 2.9 broadcast_in_dim.7.clone
  172.8 72.2 %while.11 = (s32[]{:T(128)}, f32[40,192,128]{1,2,0:T(8,128)}, s32[]{:T(128)}, bf16[40,704,128]{1,2,0:T(8,128)(2,1)}, bf16[704,40,2]{0,2,1:T(2,128)(2,1)S(1)}, /*...) while((s32[]{:T(128)}, f32[40,192,128]{1,2,0:T(8,128)}, ...), condition=%wide.region_1.2_spmd.clone, body=%wide.region_0.1_spmd.clone.sunk | while | flops 351682560 | bytes 32717972 | solution.py:39
  172.8 8.1 %broadcast_multiply_fusion.2 = bf16[704,40,2,96]{0,3,2,1:T(8,128)(2,1)} fusion(bf16[704,40,2]{0,2,1:T(2,128)(2,1)S(1)} %get-tuple-element.165, bf16[704,40,96]{0,2,1:T(8,128)(2,1)} %get-tuple-element.166), kind=kLoop, calls=%fused_computation.1.clone.1 | loop fusion | flops 5406720 | bytes 16332800 | tf_op jit(solution)/shard_map/mul | solution.py:28
  180.8 10.0 %fusion.24 = f32[40,192,128]{1,2,0:T(8,128)} fusion(f32[40,192,128]{1,2,0:T(8,128)} %get-tuple-element.152, s32[]{:T(128)S(6)} %select_n.66, bf16[704,40,192]{0,2,1:T(8,128)(2,1)} %bitcast.25, bf16[40,704,128]{1,2,0:T(8,128)(2,1)} %get-tuple-element.164), kind=kOutput, calls=%fused_computation.6.clone.1 | convolution fusion | flops 346275840 | bytes 16385024 | tf_op jit(solution)/shard_map/while/body/rpc,prl->pcl/dot_general | solution.py:35
  190.8 8.1 %broadcast_multiply_fusion.2 = bf16[704,40,2,96]{0,3,2,1:T(8,128)(2,1)} fusion(bf16[704,40,2]{0,2,1:T(2,128)(2,1)S(1)} %get-tuple-element.165, bf16[704,40,96]{0,2,1:T(8,128)(2,1)} %get-tuple-element.166), kind=kLoop, calls=%fused_computation.1.clone.1 | loop fusion | flops 5406720 | bytes 16332800 | tf_op jit(solution)/shard_map/mul | solution.py:28
  198.9 10.0 %fusion.24 = f32[40,192,128]{1,2,0:T(8,128)} fusion(f32[40,192,128]{1,2,0:T(8,128)} %get-tuple-element.152, s32[]{:T(128)S(6)} %select_n.66, bf16[704,40,192]{0,2,1:T(8,128)(2,1)} %bitcast.25, bf16[40,704,128]{1,2,0:T(8,128)(2,1)} %get-tuple-element.164), kind=kOutput, calls=%fused_computation.6.clone.1 | convolution fusion | flops 346275840 | bytes 16385024 | tf_op jit(solution)/shard_map/while/body/rpc,prl->pcl/dot_general | solution.py:35
  208.9 8.1 %broadcast_multiply_fusion.2 = bf16[704,40,2,96]{0,3,2,1:T(8,128)(2,1)} fusion(bf16[704,40,2]{0,2,1:T(2,128)(2,1)S(1)} %get-tuple-element.165, bf16[704,40,96]{0,2,1:T(8,128)(2,1)} %get-tuple-element.166), kind=kLoop, calls=%fused_computation.1.clone.1 | loop fusion | flops 5406720 | bytes 16332800 | tf_op jit(solution)/shard_map/mul | solution.py:28
  217.0 10.0 %fusion.24 = f32[40,192,128]{1,2,0:T(8,128)} fusion(f32[40,192,128]{1,2,0:T(8,128)} %get-tuple-element.152, s32[]{:T(128)S(6)} %select_n.66, bf16[704,40,192]{0,2,1:T(8,128)(2,1)} %bitcast.25, bf16[40,704,128]{1,2,0:T(8,128)(2,1)} %get-tuple-element.164), kind=kOutput, calls=%fused_computation.6.clone.1 | convolution fusion | flops 346275840 | bytes 16385024 | tf_op jit(solution)/shard_map/while/body/rpc,prl->pcl/dot_general | solution.py:35
  226.9 8.1 %broadcast_multiply_fusion.2 = bf16[704,40,2,96]{0,3,2,1:T(8,128)(2,1)} fusion(bf16[704,40,2]{0,2,1:T(2,128)(2,1)S(1)} %get-tuple-element.165, bf16[704,40,96]{0,2,1:T(8,128)(2,1)} %get-tuple-element.166), kind=kLoop, calls=%fused_computation.1.clone.1 | loop fusion | flops 5406720 | bytes 16332800 | tf_op jit(solution)/shard_map/mul | solution.py:28
  235.0 10.0 %fusion.24 = f32[40,192,128]{1,2,0:T(8,128)} fusion(f32[40,192,128]{1,2,0:T(8,128)} %get-tuple-element.152, s32[]{:T(128)S(6)} %select_n.66, bf16[704,40,192]{0,2,1:T(8,128)(2,1)} %bitcast.25, bf16[40,704,128]{1,2,0:T(8,128)(2,1)} %get-tuple-element.164), kind=kOutput, calls=%fused_computation.6.clone.1 | convolution fusion | flops 346275840 | bytes 16385024 | tf_op jit(solution)/shard_map/while/body/rpc,prl->pcl/dot_general | solution.py:35
  245.0 3.7 %copy.33 = bf16[40,192,128]{2,1,0:T(8,128)(2,1)S(1)} copy(f32[40,192,128]{1,2,0:T(8,128)} %get-tuple-element.33) | data formatting | bytes 5898240 | tf_op jit(solution)/shard_map/while | solution.py:39
  248.8 0.7 collective-permute-start
  249.5 44.0 %collective-permute-done = bf16[40,192,128]{2,1,0:T(8,128)(2,1)} collective-permute-done((bf16[40,192,128]{2,1,0:T(8,128)(2,1)S(1)}, bf16[40,192,128]{2,1,0:T(8,128)(2,1)}, u32[]{:S(2)}, u32[]{:S(2)}) %collective-permute-start) | collective-permute-done | bytes 1966112 | tf_op jit(solution)/shard_map/ppermute | solution.py:12
  293.5 2.4 fusion.16
  296.0 0.8 copy.34
  296.7 34.4 %all_to_all.18 = bf16[96,80,128]{2,1,0:T(8,128)(2,1)S(1)} all-to-all(bf16[96,80,128]{2,1,0:T(8,128)(2,1)S(1)} %copy.34), channel_id=1, replica_groups=mesh['mset'=16,'band'=16] {'mset'}, dimensions={0} | all-to-all | bytes 3932160 | tf_op jit(solution)/shard_map/all_to_all | solution.py:66
  331.2 1.4 copy.35
  (4 shorter events, 0.1 us)
Async XLA Ops:
  6.5 125.9 %all-gather.2.cloned.1.call-start = ((), (), s32[]{:S(2)}) async-start(), calls=%async_computation.1 | async-start | bytes 11489280 | tf_op jit(solution)/shard_map/all_gather | solution.py:54
  248.8 44.8 %collective-permute-start = (bf16[40,192,128]{2,1,0:T(8,128)(2,1)S(1)}, bf16[40,192,128]{2,1,0:T(8,128)(2,1)}, u32[]{:S(2)}, u32[]{:S(2)}) collective-permute-start(bf16[40,192,128]{2,1,0:T(8,128)(2,1)S(1)} %copy.33), channel_id=1, source_target_pairs={{0,1},{1,0},{2,3},{3,2},{4,5},{5,4},{6,7},{7,6},{8,9},{9,8},{10,11... | collective-permute-start | bytes 5898248 | tf_op jit(solution)/shard_map/ppermute | solution.py:12
Sparse Core Ops, SparseCore 0:
  9.1 123.2 all-gather.1
where the time goes:
time: 341 us; the launch traced here: 339 us
  waiting for transfers between devices  158 us (46%)
  local copies, waits for them, and re-layouts  56.7 us (17%)
  matrix products  40 us (12%)
  other arithmetic  35.5 us (10%)
  blocking collectives  34.4 us (10%)
  between operations  14.1 us (4%)
    all_gather x1, waiting for transfers between devices, shards(): lax.all_gather(coeffs, 'band', axis=1, tiled=True)  113 us
    ppermute x1, waiting for transfers between devices, from_partner(): return lax.ppermute(value, axis, pairs)  44 us
    dot_general x4, matrix products, one_block(): jnp.einsum('rpc,prl->pcl', stacked, columns, preferred_element_type=jnp.f...  40 us
    all_to_all x1, blocking collectives, shards(): lax.all_to_all(by_field, 'mset', split_axis=0, concat_axis=1, tiled=True)  34.4 us
    unnamed x3, local copies, waits for them, and re-layouts  34 us
    mul x4, other arithmetic, accumulate(): portion[:, :, None, :] * weights[:, :, :, None]  32.3 us
    dynamic_slice x1, local copies, waits for them, and re-layouts, shards(): lax.dynamic_index_in_dim(lax.all_gather(coeffs, 'band', axis=1, tiled=Tru...  13.9 us
  transfers between devices with their start and end apart: 2, of which 2 were waited for; matrix products, arithmetic and copies ran while one was open for 3% of the time, Pallas kernels for 0%

commit v1 on v0

v1 whole, which is shorter than its diff:
```python
import jax
import jax.numpy as jnp
from jax import lax
from jax.experimental import pallas as pl
from jax.experimental.pallas import tpu as pltpu
from jax.sharding import PartitionSpec as P

TRUNC = 1279
MESH = pl.DeviceIdType.MESH
CHUNKS = 5
GROUPS = 2
QUAD = 4
FIELDS = 96
SLOT_ROWS = 48
SLOTS = 16 * GROUPS * QUAD // 8
OFFSETS = (0, -1, 1, -2, 2, -3, 3, 4)


def first_row(band):
    return 44 * band - 4 * (band % 2)


def kernel(
    cin, first_ref, total_ref, rows_ref, legendre, out,
    held, leg, turned, stage, esend, erecv, asend,
    leg_sem, own_sem, z_send, z_recv, x_send, x_recv, e_send, e_recv, a_send, a_recv, self_sem,
):
    s = lax.axis_index("mset")
    b = lax.axis_index("band")
    xl, z = b // 8, b % 8
    parity = z % 2

    def at_z(offset):
        return lax.rem(z + (8 + offset), 8)

    def on_line(offset):
        return (s, xl * 8 + at_z(offset))

    def own_slot(offset):
        return xl * 8 + at_z(offset)

    across = (s, (1 - xl) * 8 + z)
    mirror = (s, xl * 8 + z + 1 - 2 * parity)

    barrier = pltpu.get_barrier_semaphore()
    for device in (on_line(-2), on_line(-1), on_line(1), on_line(2), across):
        pl.semaphore_signal(barrier, inc=1, device_id=device, device_id_type=MESH)

    def greet(d, carry):
        pl.semaphore_signal(barrier, inc=1, device_id=(lax.rem(s + d, 16), b), device_id_type=MESH)
        return carry

    lax.fori_loop(1, 16, greet, 0)

    def leg_copy(k):
        pairs = pl.ds(k * GROUPS * QUAD, GROUPS * QUAD)
        return pltpu.make_async_copy(legendre.at[pairs], leg.at[pairs], leg_sem.at[k])

    for k in range(CHUNKS):
        leg_copy(k).start()
    own_copy = pltpu.make_async_copy(cin.at[parity], held.at[own_slot(0)], own_sem)
    own_copy.start()
    pl.semaphore_wait(barrier, 20)

    def whole(k):
        return pl.ds(k * GROUPS, GROUPS)

    def half(k, i):
        return pl.ds(k * GROUPS + i * (GROUPS // 2), GROUPS // 2)

    def z_copy(kind, k):
        if kind == 0:
            src, block, target, cols = cin.at[parity, whole(k)], 0, 2, whole(k)
        elif kind == 1:
            src, block, target, cols = cin.at[parity, whole(k)], 0, -2, whole(k)
        elif kind == 2:
            src, block, target, cols = cin.at[1 - parity, whole(k)], 0, 1, whole(k)
        elif kind == 3:
            src, block, target, cols = cin.at[1 - parity, whole(k)], 0, -1, whole(k)
        else:
            block, target, cols = {
                4: (-1, 2, whole(k)),
                5: (1, -2, whole(k)),
                6: (-2, 2, half(k, 0)),
                7: (2, -2, half(k, 1)),
            }[kind]
            src = held.at[own_slot(block), cols]
        return pltpu.make_async_remote_copy(
            src_ref=src,
            dst_ref=held.at[own_slot(block), cols],
            send_sem=z_send.at[kind, k],
            recv_sem=z_recv.at[kind, k],
            device_id=on_line(target),
            device_id_type=MESH,
        )

    def z_arrival(kind, k):
        block, cols = {
            0: (-2, whole(k)),
            1: (2, whole(k)),
            2: (-1, whole(k)),
            3: (1, whole(k)),
            4: (-3, whole(k)),
            5: (3, whole(k)),
            6: (4, half(k, 0)),
            7: (4, half(k, 1)),
        }[kind]
        here = held.at[own_slot(block), cols]
        return pltpu.make_async_copy(here, here, z_recv.at[kind, k])

    def x_copy(j, k):
        slot = own_slot(OFFSETS[j])
        src = cin.at[parity, whole(k)] if j == 0 else held.at[slot, whole(k)]
        return pltpu.make_async_remote_copy(
            src_ref=src,
            dst_ref=held.at[slot, whole(k)],
            send_sem=x_send.at[j, k],
            recv_sem=x_recv.at[j, k],
            device_id=across,
            device_id_type=MESH,
        )

    def x_arrival(j, k):
        here = held.at[(1 - xl) * 8 + at_z(OFFSETS[j]), whole(k)]
        return pltpu.make_async_copy(here, here, x_recv.at[j, k])

    def e_copy(k):
        return pltpu.make_async_remote_copy(
            src_ref=esend.at[k],
            dst_ref=erecv.at[k],
            send_sem=e_send.at[k],
            recv_sem=e_recv.at[k],
            device_id=mirror,
            device_id_type=MESH,
        )

    def out_rows(k):
        return pl.ds(pl.multiple_of(s * (CHUNKS * SLOTS) + k * SLOTS, SLOTS), SLOTS)

    def self_copy(k):
        return pltpu.make_async_copy(asend.at[k, pl.ds(s * 6, 6)], out.at[:, out_rows(k), :], self_sem.at[k])

    def direct(k):
        for kind in range(4):
            z_copy(kind, k).start()
        x_copy(0, k).start()

    def forward(k):
        for kind in (2, 3, 0, 1):
            z_arrival(kind, k).wait()
            z_copy({2: 4, 3: 5, 0: 6, 1: 7}[kind], k).start()
            x_copy({2: 1, 3: 2, 0: 3, 1: 4}[kind], k).start()

    def last(k):
        z_arrival(4, k).wait()
        x_copy(5, k).start()
        z_arrival(5, k).wait()
        x_copy(6, k).start()
        z_arrival(6, k).wait()
        z_arrival(7, k).wait()
        x_copy(7, k).start()

    def transform(k):
        for j in range(8):
            x_arrival(j, k).wait()
        leg_copy(k).wait()

        def group(i, carry):
            g = k * GROUPS + i
            turned[...] = held[:, g].reshape(16 * SLOT_ROWS, QUAD * FIELDS).T
            for n in range(QUAD):
                q = g * QUAD + n
                first, total = first_ref[q], total_ref[q]
                low, high = [], []
                for band in range(16):
                    row = lax.broadcasted_iota(jnp.int32, (SLOT_ROWS, 128), 0) + first_row(band)
                    piece = leg[q, pl.ds(first_row(band), SLOT_ROWS), :]
                    zero = jnp.zeros_like(piece)
                    low.append(jnp.where(row < first, piece, zero))
                    high.append(jnp.where((row >= first) & (row < total), piece, zero))
                basis = jnp.concatenate([jnp.concatenate(low, 0), jnp.concatenate(high, 0)], 1)
                sums = jnp.dot(
                    turned[pl.ds(n * FIELDS, FIELDS), :], basis, preferred_element_type=jnp.float32
                )
                slot = i * (2 * QUAD) + 2 * n
                stage[pl.ds(slot, FIELDS, stride=SLOTS), :] = sums[:, :128]
                stage[pl.ds(slot + 1, FIELDS, stride=SLOTS), :] = sums[:, 128:]
            return carry

        lax.fori_loop(0, GROUPS, group, 0)
        esend[k] = stage[...].astype(jnp.bfloat16).reshape(FIELDS, SLOTS, 128)
        e_copy(k).start()

    def combine(k):
        e_copy(k).wait_recv()
        own = esend[k].astype(jnp.float32)
        partner = erecv[k].astype(jnp.float32)
        sign = jnp.where(parity == 0, 1.0, -1.0).astype(jnp.float32)
        grid = partner + sign * own
        lane = lax.broadcasted_iota(jnp.int32, grid.shape, 2)
        asend[k] = jnp.where(lane < rows_ref[0], grid, 0.0).astype(jnp.bfloat16)
        self_copy(k).start()

        def send(d, carry):
            t = lax.rem(s + d, 16)
            pltpu.make_async_remote_copy(
                src_ref=asend.at[k, pl.ds(t * 6, 6)],
                dst_ref=out.at[:, out_rows(k), :],
                send_sem=a_send,
                recv_sem=a_recv,
                device_id=(t, b),
                device_id_type=MESH,
            ).start()
            return carry

        lax.fori_loop(1, 16, send, 0)

    own_copy.wait()

    def step(i, carry):
        for delay, stage_of in enumerate((direct, forward, last, transform, combine)):
            k = i - delay

            @pl.when((k >= 0) & (k < CHUNKS))
            def _(k=k, stage_of=stage_of):
                stage_of(k)

        return carry

    lax.fori_loop(0, CHUNKS + 4, step, 0)

    def finish(k, carry):
        for kind in range(8):
            z_copy(kind, k).wait_send()
        for j in range(8):
            x_copy(j, k).wait_send()
        e_copy(k).wait_send()
        self_copy(k).wait()
        return carry

    lax.fori_loop(0, CHUNKS, finish, 0)
    sent = asend.at[:, pl.ds(0, 90)]
    pltpu.make_async_copy(sent, sent, a_send).wait()
    got = out.at[:, pl.ds(0, 15 * CHUNKS * SLOTS), :]
    pltpu.make_async_copy(got, got, a_recv).wait()


def shards(coeffs, legendre, wavenumber, band_rows):
    band = lax.axis_index("band")
    parity = band % 2
    first = jnp.maximum((TRUNC - wavenumber - parity) // 2 + 1, 0)
    total = first + jnp.maximum((wavenumber - parity) // 2 + 1, 0)
    blocks = CHUNKS * GROUPS
    split = jnp.swapaxes(coeffs.reshape(2, 44, blocks, QUAD * FIELDS), 1, 2)
    pads = [jnp.pad(split, ((0, 0), (0, 0), ends, (0, 0))) for ends in ((0, 4), (4, 0))]
    cin = jnp.where(parity == 0, pads[0], pads[1])
    vmem = pl.BlockSpec(memory_space=pltpu.VMEM)
    smem = pl.BlockSpec(memory_space=pltpu.SMEM)
    anywhere = pl.BlockSpec(memory_space=pl.ANY)
    dma = pltpu.SemaphoreType.DMA
    sums = (CHUNKS, FIELDS, SLOTS, 128)
    return pl.pallas_call(
        kernel,
        out_shape=jax.ShapeDtypeStruct((6, 16 * CHUNKS * SLOTS, 128), jnp.bfloat16),
        in_specs=[vmem, smem, smem, smem, anywhere],
        out_specs=anywhere,
        scratch_shapes=[
            pltpu.VMEM((16, blocks, SLOT_ROWS, QUAD * FIELDS), jnp.bfloat16),
            pltpu.VMEM(legendre.shape, jnp.bfloat16),
            pltpu.VMEM((QUAD * FIELDS, 16 * SLOT_ROWS), jnp.bfloat16),
            pltpu.VMEM((FIELDS * SLOTS, 128), jnp.float32),
            pltpu.VMEM(sums, jnp.bfloat16),
            pltpu.VMEM(sums, jnp.bfloat16),
            pltpu.VMEM(sums, jnp.bfloat16),
            dma((CHUNKS,)),
            dma,
            dma((8, CHUNKS)),
            dma((8, CHUNKS)),
            dma((8, CHUNKS)),
            dma((8, CHUNKS)),
            dma((CHUNKS,)),
            dma((CHUNKS,)),
            dma,
            dma,
            dma((CHUNKS,)),
        ],
        compiler_params=pltpu.CompilerParams(
            collective_id=0, has_side_effects=True, vmem_limit_bytes=48 * 1024 * 1024
        ),
        cost_estimate=pl.CostEstimate(
            flops=2 * 40 * 768 * 96 * 256, bytes_accessed=20_000_000, transcendentals=0
        ),
    )(cin, first, total, band_rows, legendre)


def solution(mesh):
    in_specs = (P(None, "band", "mset"), P("mset", None, "band"), P("mset"), P("band"))
    out_specs = P("mset", None, "band")
    return jax.shard_map(shards, mesh=mesh, in_specs=in_specs, out_specs=out_specs, check_vma=False)
```

time: 341 us -> 114 us (0.33)
  the two profiles are of different devices: /device:TPU:192 before, /device:TPU:1 now
where the time goes in v1:
time: 114 us
  Pallas kernels  109 us (96%)
  local copies, waits for them, and re-layouts  3.75 us (3%)
    pallas_call x1, Pallas kernels, shards(): pl.pallas_call(kernel, out_shape=jax.ShapeDtypeStruct((6, 16 * CHUNKS * S...  109 us
    reshape x2, local copies, waits for them, and re-layouts, shards(): split = jnp.swapaxes(coeffs.reshape(2, 44, blocks, QUAD * FIELDS), 1, 2)  2.48 us

profile of v1, /device:TPU:1, one launch (start us, length us, event | category | flops | bytes accessed | tf_op | source)
XLA Modules:
  0.0 114.3 jit_solution(1909826041291050600)
XLA Ops:
  0.7 0.7 maximum_add_fusion
  1.3 2.3 %reshape.3 = bf16[2,44,10,384]{3,2,0,1:T(8,128)(2,1)S(1)} reshape(bf16[2,44,3840]{2,0,1:T(2,128)(2,1)} %param.4) | data formatting | bytes 1351680 | tf_op jit(solution)/shard_map/reshape | solution.py:254
  3.6 0.2 copy.7
  3.8 0.2 pad_select_fusion.cin
  4.1 108.9 %shard_map.46 = bf16[6,1280,128]{2,1,0:T(8,128)(2,1)S(1)} custom-call(bf16[2,10,48,384]{3,2,1,0:T(8,128)(2,1)S(1)} %pad_select_fusion.cin, s32[40]{0:T(128)S(1)} %get-tuple-element.6.first_ref, s32[40]{0:T(128)S(1)} %get-tuple-element.5.total_ref, s32[1]{0:T(128)S(6)} %copy.9.rows_ref, bf16[40,704,128]{2,1,0:T(8,128)(2,1)} %legendre.1), custom_call_target="tpu_custom_call" | custom-call | flops 1509949440 | bytes 20000000 | tf_op jit(solution)/shard_map/pallas_call | solution.py:262
  113.0 1.3 %copy.10 = bf16[6,1280,128]{2,1,0:T(8,128)(2,1)} copy(bf16[6,1280,128]{2,1,0:T(8,128)(2,1)S(1)} %shard_map.46) | data formatting | bytes 3932160

commit v2 on v1

v2 whole, which is shorter than its diff:
```python
import jax
import jax.numpy as jnp
from jax import lax
from jax.experimental import pallas as pl
from jax.experimental.pallas import tpu as pltpu
from jax.sharding import PartitionSpec as P

TRUNC = 1279
MESH = pl.DeviceIdType.MESH
CHUNKS = 5
GROUPS = 2
QUAD = 4
FIELDS = 96
ROWS = 704
MAIN = 40
BLOCK = 2 * MAIN + 8
SLOTS = 2 * GROUPS * QUAD
PIECES = 4
OFFSETS = (0, -1, 1, -2, 2, -3, 3, 4)


def kernel(
    cin, first_ref, total_ref, rows_ref, legendre, out,
    held, leg, natural, turned, stage, esend, erecv, asend,
    leg_sem, own_sem, z_send, z_recv, x_send, x_recv, e_send, e_recv, a_send, a_recv, self_sem,
):
    s = lax.axis_index("mset")
    b = lax.axis_index("band")
    xl, z = b // 8, b % 8
    parity = z % 2

    def at_z(offset):
        return lax.rem(z + (8 + offset), 8)

    def on_line(offset):
        return (s, xl * 8 + at_z(offset))

    def own_slot(offset):
        return xl * 8 + at_z(offset)

    across = (s, (1 - xl) * 8 + z)
    mirror = (s, xl * 8 + z + 1 - 2 * parity)

    barrier = pltpu.get_barrier_semaphore()
    for device in (on_line(-2), on_line(-1), on_line(1), on_line(2), across):
        pl.semaphore_signal(barrier, inc=1, device_id=device, device_id_type=MESH)

    def greet(d, carry):
        pl.semaphore_signal(barrier, inc=1, device_id=(lax.rem(s + d, 16), b), device_id_type=MESH)
        return carry

    lax.fori_loop(1, 16, greet, 0)

    def leg_copy(k):
        pairs = pl.ds(k * GROUPS * QUAD, GROUPS * QUAD)
        return pltpu.make_async_copy(legendre.at[pairs], leg.at[pairs], leg_sem.at[k])

    for k in range(CHUNKS):
        leg_copy(k).start()
    own_copy = pltpu.make_async_copy(cin.at[parity], held.at[own_slot(0)], own_sem)
    own_copy.start()
    pl.semaphore_wait(barrier, 20)

    def z_copy(kind, k):
        if kind == 4:
            way = 1 - 2 * lax.rem(k + s, 2)
            block, target = -2 * way, 2 * way
        else:
            block, target = {0: (0, 2), 1: (0, -2), 2: (0, 1), 3: (0, -1), 5: (-1, 2), 6: (1, -2)}[kind]
        if kind in (0, 1):
            src = cin.at[parity, k]
        elif kind in (2, 3):
            src = cin.at[1 - parity, k]
        else:
            src = held.at[own_slot(block), k]
        return pltpu.make_async_remote_copy(
            src_ref=src,
            dst_ref=held.at[own_slot(block), k],
            send_sem=z_send.at[kind, k],
            recv_sem=z_recv.at[kind, k],
            device_id=on_line(target),
            device_id_type=MESH,
        )

    def z_arrival(kind, k):
        block = {0: -2, 1: 2, 2: -1, 3: 1, 4: 4, 5: -3, 6: 3}[kind]
        here = held.at[own_slot(block), k]
        return pltpu.make_async_copy(here, here, z_recv.at[kind, k])

    def x_copy(j, k):
        slot = own_slot(OFFSETS[j])
        return pltpu.make_async_remote_copy(
            src_ref=cin.at[parity, k] if j == 0 else held.at[slot, k],
            dst_ref=held.at[slot, k],
            send_sem=x_send.at[j, k],
            recv_sem=x_recv.at[j, k],
            device_id=across,
            device_id_type=MESH,
        )

    def x_arrival(j, k):
        here = held.at[(1 - xl) * 8 + at_z(OFFSETS[j]), k]
        return pltpu.make_async_copy(here, here, x_recv.at[j, k])

    def e_copy(k, piece):
        return pltpu.make_async_remote_copy(
            src_ref=esend.at[k, piece],
            dst_ref=erecv.at[k, piece],
            send_sem=e_send.at[k, piece],
            recv_sem=e_recv.at[k, piece],
            device_id=mirror,
            device_id_type=MESH,
        )

    def out_rows(k):
        return pl.ds(pl.multiple_of(s * (CHUNKS * SLOTS) + k * SLOTS, SLOTS), SLOTS)

    def self_copy(k):
        return pltpu.make_async_copy(asend.at[k, pl.ds(s * 6, 6)], out.at[:, out_rows(k), :], self_sem.at[k])

    def direct(k):
        for kind in range(4):
            z_copy(kind, k).start()
        x_copy(0, k).start()

    def forward(k):
        for kind in (2, 3, 0, 1):
            z_arrival(kind, k).wait()
            if kind >= 2:
                z_copy(kind + 3, k).start()
            x_copy({2: 1, 3: 2, 0: 3, 1: 4}[kind], k).start()
        z_copy(4, k).start()

    def last(k):
        for kind, j in ((5, 5), (6, 6), (4, 7)):
            z_arrival(kind, k).wait()
            x_copy(j, k).start()

    def transform(k):
        for j in range(8):
            x_arrival(j, k).wait()
        leg_copy(k).wait()
        row = lax.broadcasted_iota(jnp.int32, (ROWS, 128), 0)
        upper = lax.broadcasted_iota(jnp.int32, (8, QUAD * FIELDS), 0) < 4
        for i in range(GROUPS):
            for j in range(8):
                start = j * 2 * 44
                for band, place in ((2 * j, start), (2 * j + 1, start + MAIN + 8)):
                    natural[pl.ds(place, MAIN), :] = held[band, k, pl.ds(i * MAIN, MAIN), :]
                tails = [held[band, k, pl.ds(2 * MAIN, 8), :].astype(jnp.float32) for band in (2 * j, 2 * j + 1)]
                if i == 0:
                    shared = jnp.where(upper, tails[0], tails[1])
                else:
                    shared = pltpu.roll(jnp.where(upper, tails[1], tails[0]), 4, 0)
                natural[pl.ds(start + MAIN, 8), :] = shared.astype(jnp.bfloat16)
            turned[...] = natural[...].T

            def pair(n, carry, i=i):
                q = (k * GROUPS + i) * QUAD + n
                first, total = first_ref[q], total_ref[q]
                values = leg[q]
                zero = jnp.zeros_like(values)
                low = jnp.where(row < first, values, zero)
                high = jnp.where((row >= first) & (row < total), values, zero)
                fields = turned[pl.ds(pl.multiple_of(n * FIELDS, FIELDS), FIELDS), :]
                sums = jnp.dot(
                    fields, jnp.concatenate([low, high], 1), preferred_element_type=jnp.float32
                )
                slot = i * (2 * QUAD) + 2 * n
                stage[pl.ds(slot, FIELDS, stride=SLOTS), :] = sums[:, :128]
                stage[pl.ds(slot + 1, FIELDS, stride=SLOTS), :] = sums[:, 128:]
                return carry

            lax.fori_loop(0, QUAD, pair, 0)
        esend[k] = stage[...].astype(jnp.bfloat16).reshape(esend.shape[1:])
        for j in range(PIECES):
            e_copy(k, piece_of(j)).start()

    def piece_of(j):
        return lax.rem(s // 4 + 1 + j, PIECES)

    def combine(k):
        sign = jnp.where(parity == 0, 1.0, -1.0).astype(jnp.float32)
        lane = lax.broadcasted_iota(jnp.int32, esend.shape[2:], 2)

        def part(j, carry):
            piece = piece_of(j)
            e_copy(k, piece).wait_recv()
            grid = erecv[k, piece].astype(jnp.float32) + sign * esend[k, piece].astype(jnp.float32)
            columns = pl.ds(piece * (FIELDS // PIECES), FIELDS // PIECES)
            asend[k, columns] = jnp.where(lane < rows_ref[0], grid, 0.0).astype(jnp.bfloat16)

            def send(d, carry):
                t = piece * 4 + lax.rem(s + d, 4)

                @pl.when(t != s)
                def _():
                    pltpu.make_async_remote_copy(
                        src_ref=asend.at[k, pl.ds(t * 6, 6)],
                        dst_ref=out.at[:, out_rows(k), :],
                        send_sem=a_send,
                        recv_sem=a_recv,
                        device_id=(t, b),
                        device_id_type=MESH,
                    ).start()

                @pl.when(t == s)
                def _():
                    self_copy(k).start()

                return carry

            return lax.fori_loop(0, 4, send, carry)

        lax.fori_loop(0, PIECES, part, 0)

    own_copy.wait()

    def begin(k, carry):
        direct(k)
        return carry

    lax.fori_loop(0, 1, begin, 0)

    def step(i, carry):
        @pl.when(i + 1 < CHUNKS)
        def _():
            direct(i + 1)

        for delay, stage_of in ((0, forward), (1, last), (2, transform), (3, combine)):
            k = i - delay

            @pl.when((k >= 0) & (k < CHUNKS))
            def _(k=k, stage_of=stage_of):
                stage_of(k)

        return carry

    lax.fori_loop(0, CHUNKS + 3, step, 0)

    def finish(k, carry):
        for kind in range(7):
            z_copy(kind, k).wait_send()
        for j in range(8):
            x_copy(j, k).wait_send()
        for j in range(PIECES):
            e_copy(k, j).wait_send()
        self_copy(k).wait()
        return carry

    lax.fori_loop(0, CHUNKS, finish, 0)
    sent = asend.at[:, pl.ds(0, 90)]
    pltpu.make_async_copy(sent, sent, a_send).wait()
    got = out.at[:, pl.ds(0, 15 * CHUNKS * SLOTS), :]
    pltpu.make_async_copy(got, got, a_recv).wait()


def shards(coeffs, legendre, wavenumber, band_rows):
    band = lax.axis_index("band")
    parity = band % 2
    first = jnp.maximum((TRUNC - wavenumber - parity) // 2 + 1, 0)
    total = first + jnp.maximum((wavenumber - parity) // 2 + 1, 0)
    split = coeffs.reshape(2, 44, CHUNKS, GROUPS, QUAD * FIELDS)
    main = jnp.where(parity == 0, split[:, :MAIN], split[:, 4:])
    tail = jnp.where(parity == 0, split[:, MAIN:], split[:, :4, :, ::-1])
    cin = jnp.concatenate(
        [part.transpose(0, 2, 3, 1, 4).reshape(2, CHUNKS, -1, QUAD * FIELDS) for part in (main, tail)], 2
    )
    vmem = pl.BlockSpec(memory_space=pltpu.VMEM)
    smem = pl.BlockSpec(memory_space=pltpu.SMEM)
    anywhere = pl.BlockSpec(memory_space=pl.ANY)
    dma = pltpu.SemaphoreType.DMA
    sums = (CHUNKS, PIECES, FIELDS // PIECES, SLOTS, 128)
    return pl.pallas_call(
        kernel,
        out_shape=jax.ShapeDtypeStruct((6, 16 * CHUNKS * SLOTS, 128), jnp.bfloat16),
        in_specs=[vmem, smem, smem, smem, anywhere],
        out_specs=anywhere,
        scratch_shapes=[
            pltpu.VMEM((16, CHUNKS, BLOCK, QUAD * FIELDS), jnp.bfloat16),
            pltpu.VMEM(legendre.shape, jnp.bfloat16),
            pltpu.VMEM((ROWS, QUAD * FIELDS), jnp.bfloat16),
            pltpu.VMEM((QUAD * FIELDS, ROWS), jnp.bfloat16),
            pltpu.VMEM((FIELDS * SLOTS, 128), jnp.float32),
            pltpu.VMEM(sums, jnp.bfloat16),
            pltpu.VMEM(sums, jnp.bfloat16),
            pltpu.VMEM((CHUNKS, FIELDS, SLOTS, 128), jnp.bfloat16),
            dma((CHUNKS,)),
            dma,
            dma((7, CHUNKS)),
            dma((7, CHUNKS)),
            dma((8, CHUNKS)),
            dma((8, CHUNKS)),
            dma((CHUNKS, PIECES)),
            dma((CHUNKS, PIECES)),
            dma,
            dma,
            dma((CHUNKS,)),
        ],
        compiler_params=pltpu.CompilerParams(
            collective_id=0, has_side_effects=True, vmem_limit_bytes=48 * 1024 * 1024
        ),
        cost_estimate=pl.CostEstimate(
            flops=2 * 40 * ROWS * 96 * 256, bytes_accessed=20_000_000, transcendentals=0
        ),
    )(cin, first, total, band_rows, legendre)


def solution(mesh):
    in_specs = (P(None, "band", "mset"), P("mset", None, "band"), P("mset"), P("band"))
    out_specs = P("mset", None, "band")
    return jax.shard_map(shards, mesh=mesh, in_specs=in_specs, out_specs=out_specs, check_vma=False)
```

time: 114 us -> 108 us (0.947)
  Pallas kernels: 109 us -> 102 us
    pallas_call x1, Pallas kernels: 109 us -> 102 us  [shards(): pl.pallas_call(kernel, out_shape=jax.ShapeDtypeStruct((6, 16 * CHUNKS * S...]
where the time goes in v2:
time: 108 us
  Pallas kernels  102 us (94%)
  local copies, waits for them, and re-layouts  4.72 us (4%)
    pallas_call x1, Pallas kernels, shards(): pl.pallas_call(kernel, out_shape=jax.ShapeDtypeStruct((6, 16 * CHUNKS * S...  102 us
    reshape x1, local copies, waits for them, and re-layouts, shards(): split = coeffs.reshape(2, 44, CHUNKS, GROUPS, QUAD * FIELDS)  2.65 us

profile of v2, /device:TPU:1, one launch (start us, length us, event | category | flops | bytes accessed | tf_op | source)
XLA Modules:
  0.0 108.1 jit_solution(2316494358800626497)
XLA Ops:
  0.7 0.7 maximum_add_fusion
  1.3 2.6 %reshape.9 = bf16[2,44,5,2,384]{4,3,2,0,1:T(2,128)(2,1)S(1)} reshape(bf16[2,44,3840]{2,0,1:T(2,128)(2,1)} %param.4) | data formatting | bytes 1351680 | tf_op jit(solution)/shard_map/reshape | solution.py:263
  4.0 0.1 fusion.2
  4.2 0.7 fusion.1
  4.8 0.2 copy_select_fusion
  5.0 0.1 pad_maximum_fusion.cin
  5.1 101.7 %shard_map.46 = bf16[6,1280,128]{2,1,0:T(8,128)(2,1)S(1)} custom-call(bf16[2,5,88,384]{3,2,1,0:T(8,128)(2,1)S(1)} %pad_maximum_fusion.cin, s32[40]{0:T(128)S(1)} %get-tuple-element.6.first_ref, s32[40]{0:T(128)S(1)} %get-tuple-element.5.total_ref, s32[1]{0:T(128)S(6)} %copy.19.rows_ref, bf16[40,704,128]{2,1,0:T(8,128)(2,1)} %legendre.1), custom_call_target="tpu_custom_call" | custom-call | flops 1384120320 | bytes 20000000 | tf_op jit(solution)/shard_map/pallas_call | solution.py:274
  106.8 1.3 %copy.20 = bf16[6,1280,128]{2,1,0:T(8,128)(2,1)} copy(bf16[6,1280,128]{2,1,0:T(8,128)(2,1)S(1)} %shard_map.46) | data formatting | bytes 3932160
  (3 shorter events, 0.1 us)

commit v3 on v2

--- a/solution.py
+++ b/solution.py
@@ -15,14 +15,15 @@
 MAIN = 40
 BLOCK = 2 * MAIN + 8
 SLOTS = 2 * GROUPS * QUAD
-PIECES = 4
+PIECES = 8
+PEERS = 16 // PIECES
 OFFSETS = (0, -1, 1, -2, 2, -3, 3, 4)
 
 
 def kernel(
-    cin, first_ref, total_ref, rows_ref, legendre, out,
-    held, leg, natural, turned, stage, esend, erecv, asend,
-    leg_sem, own_sem, z_send, z_recv, x_send, x_recv, e_send, e_recv, a_send, a_recv, self_sem,
+    coeffs, wave_ref, rows_ref, legendre, out,
+    raw, other, held, leg, natural, turned, stage, esend, erecv, asend,
+    leg_sem, raw_sem, z_send, z_recv, x_send, x_recv, e_send, e_recv, a_send, a_recv, self_sem,
 ):
     s = lax.axis_index("mset")
     b = lax.axis_index("band")
@@ -55,10 +56,42 @@
         pairs = pl.ds(k * GROUPS * QUAD, GROUPS * QUAD)
         return pltpu.make_async_copy(legendre.at[pairs], leg.at[pairs], leg_sem.at[k])
 
+    raw_copy = pltpu.make_async_copy(coeffs, raw, raw_sem)
+    raw_copy.start()
     for k in range(CHUNKS):
         leg_copy(k).start()
-    own_copy = pltpu.make_async_copy(cin.at[parity], held.at[own_slot(0)], own_sem)
-    own_copy.start()
+    raw_copy.wait()
+
+    def pack(k):
+        both = []
+        for i in range(GROUPS):
+            start = pl.multiple_of((k * GROUPS + i) * (QUAD * FIELDS), QUAD * FIELDS)
+            both.append(raw[:, :, pl.ds(start, QUAD * FIELDS)].astype(jnp.float32))
+
+        def fill(put, p):
+            parts = [values[:, p, :] for values in both]
+            if parity_of == 0:
+                mains, tails = [v[:MAIN] for v in parts], [v[MAIN:] for v in parts]
+            else:
+                mains, tails = [v[4:] for v in parts], [v[:4] for v in reversed(parts)]
+            put(0, mains[0])
+            put(MAIN, mains[1])
+            put(2 * MAIN, jnp.concatenate(tails, 0))
+
+        def put_own(row, values):
+            held[own_slot(0), k, pl.ds(row, values.shape[0]), :] = values.astype(jnp.bfloat16)
+
+        def put_other(row, values):
+            other[k, pl.ds(row, values.shape[0]), :] = values.astype(jnp.bfloat16)
+
+        for parity_of in range(2):
+
+            @pl.when(parity == parity_of)
+            def _():
+                fill(put_own, parity_of)
+                fill(put_other, 1 - parity_of)
+
+    pack(0)
     pl.semaphore_wait(barrier, 20)
 
     def z_copy(kind, k):
@@ -67,12 +100,7 @@
             block, target = -2 * way, 2 * way
         else:
             block, target = {0: (0, 2), 1: (0, -2), 2: (0, 1), 3: (0, -1), 5: (-1, 2), 6: (1, -2)}[kind]
-        if kind in (0, 1):
-            src = cin.at[parity, k]
-        elif kind in (2, 3):
-            src = cin.at[1 - parity, k]
-        else:
-            src = held.at[own_slot(block), k]
+        src = other.at[k] if kind in (2, 3) else held.at[own_slot(block), k]
         return pltpu.make_async_remote_copy(
             src_ref=src,
             dst_ref=held.at[own_slot(block), k],
@@ -90,7 +118,7 @@
     def x_copy(j, k):
         slot = own_slot(OFFSETS[j])
         return pltpu.make_async_remote_copy(
-            src_ref=cin.at[parity, k] if j == 0 else held.at[slot, k],
+            src_ref=held.at[slot, k],
             dst_ref=held.at[slot, k],
             send_sem=x_send.at[j, k],
             recv_sem=x_recv.at[j, k],
@@ -157,7 +185,9 @@
 
             def pair(n, carry, i=i):
                 q = (k * GROUPS + i) * QUAD + n
-                first, total = first_ref[q], total_ref[q]
+                m = wave_ref[q]
+                first = jnp.maximum(lax.shift_right_arithmetic(TRUNC - m - parity, 1) + 1, 0)
+                total = first + jnp.maximum(lax.shift_right_arithmetic(m - parity, 1) + 1, 0)
                 values = leg[q]
                 zero = jnp.zeros_like(values)
                 low = jnp.where(row < first, values, zero)
@@ -177,7 +207,7 @@
             e_copy(k, piece_of(j)).start()
 
     def piece_of(j):
-        return lax.rem(s // 4 + 1 + j, PIECES)
+        return lax.rem(s // PEERS + 1 + j, PIECES)
 
     def combine(k):
         sign = jnp.where(parity == 0, 1.0, -1.0).astype(jnp.float32)
@@ -191,7 +221,7 @@
             asend[k, columns] = jnp.where(lane < rows_ref[0], grid, 0.0).astype(jnp.bfloat16)
 
             def send(d, carry):
-                t = piece * 4 + lax.rem(s + d, 4)
+                t = piece * PEERS + lax.rem(s + 1 + d, PEERS)
 
                 @pl.when(t != s)
                 def _():
@@ -210,39 +240,36 @@
 
                 return carry
 
-            return lax.fori_loop(0, 4, send, carry)
+            return lax.fori_loop(0, PEERS, send, carry)
 
         lax.fori_loop(0, PIECES, part, 0)
 
-    own_copy.wait()
-
-    def begin(k, carry):
-        direct(k)
-        return carry
-
-    lax.fori_loop(0, 1, begin, 0)
-
-    def step(i, carry):
-        @pl.when(i + 1 < CHUNKS)
-        def _():
-            direct(i + 1)
-
-        for delay, stage_of in ((0, forward), (1, last), (2, transform), (3, combine)):
-            k = i - delay
-
-            @pl.when((k >= 0) & (k < CHUNKS))
-            def _(k=k, stage_of=stage_of):
-                stage_of(k)
-
-        return carry
-
-    lax.fori_loop(0, CHUNKS + 3, step, 0)
-
-    def finish(k, carry):
+    direct(0)
+
+    def drain(k):
         for kind in range(7):
             z_copy(kind, k).wait_send()
         for j in range(8):
             x_copy(j, k).wait_send()
+
+    def step(i, carry):
+        @pl.when(i + 1 < CHUNKS)
+        def _():
+            pack(i + 1)
+            direct(i + 1)
+
+        for delay, stage_of in ((0, forward), (1, last), (2, transform), (3, drain), (3, combine)):
+            k = i - delay
+
+            @pl.when((k >= 0) & (k < CHUNKS))
+            def _(k=k, stage_of=stage_of):
+                stage_of(k)
+
+        return carry
+
+    lax.fori_loop(0, CHUNKS + 3, step, 0)
+
+    def finish(k, carry):
         for j in range(PIECES):
             e_copy(k, j).wait_send()
         self_copy(k).wait()
@@ -256,17 +283,6 @@
 
 
 def shards(coeffs, legendre, wavenumber, band_rows):
-    band = lax.axis_index("band")
-    parity = band % 2
-    first = jnp.maximum((TRUNC - wavenumber - parity) // 2 + 1, 0)
-    total = first + jnp.maximum((wavenumber - parity) // 2 + 1, 0)
-    split = coeffs.reshape(2, 44, CHUNKS, GROUPS, QUAD * FIELDS)
-    main = jnp.where(parity == 0, split[:, :MAIN], split[:, 4:])
-    tail = jnp.where(parity == 0, split[:, MAIN:], split[:, :4, :, ::-1])
-    cin = jnp.concatenate(
-        [part.transpose(0, 2, 3, 1, 4).reshape(2, CHUNKS, -1, QUAD * FIELDS) for part in (main, tail)], 2
-    )
-    vmem = pl.BlockSpec(memory_space=pltpu.VMEM)
     smem = pl.BlockSpec(memory_space=pltpu.SMEM)
     anywhere = pl.BlockSpec(memory_space=pl.ANY)
     dma = pltpu.SemaphoreType.DMA
@@ -274,9 +290,11 @@
     return pl.pallas_call(
         kernel,
         out_shape=jax.ShapeDtypeStruct((6, 16 * CHUNKS * SLOTS, 128), jnp.bfloat16),
-        in_specs=[vmem, smem, smem, smem, anywhere],
+        in_specs=[anywhere, smem, smem, anywhere],
         out_specs=anywhere,
         scratch_shapes=[
+            pltpu.VMEM((44, 2, coeffs.shape[2]), jnp.bfloat16),
+            pltpu.VMEM((CHUNKS, BLOCK, QUAD * FIELDS), jnp.bfloat16),
             pltpu.VMEM((16, CHUNKS, BLOCK, QUAD * FIELDS), jnp.bfloat16),
             pltpu.VMEM(legendre.shape, jnp.bfloat16),
             pltpu.VMEM((ROWS, QUAD * FIELDS), jnp.bfloat16),
@@ -303,7 +321,7 @@
         cost_estimate=pl.CostEstimate(
             flops=2 * 40 * ROWS * 96 * 256, bytes_accessed=20_000_000, transcendentals=0
         ),
-    )(cin, first, total, band_rows, legendre)
+    )(jnp.swapaxes(coeffs, 0, 1), wavenumber, band_rows, legendre)
 
 
 def solution(mesh):

time: 108 us -> 105 us (0.972)
  local copies, waits for them, and re-layouts: 4.72 us -> 3.02 us
    reshape x2 -> x0, local copies, waits for them, and re-layouts: 2.67 us -> none  [the longest x1 2.65 us: shards(): split = coeffs.reshape(2, 44, CHUNKS, GROUPS, QUAD * FIELDS)]
    unnamed x2 -> x5, local copies, waits for them, and re-layouts: 1.3 us -> 3.02 us
where the time goes in v3:
time: 105 us; the launch traced here: 104 us
  Pallas kernels  101 us (96%)
  local copies, waits for them, and re-layouts  3.02 us (3%)
    pallas_call x1, Pallas kernels, shards(): pl.pallas_call(kernel, out_shape=jax.ShapeDtypeStruct((6, 16 * CHUNKS * S...  101 us
    unnamed x5, local copies, waits for them, and re-layouts  3.02 us

profile of v3, /device:TPU:1, one launch (start us, length us, event | category | flops | bytes accessed | tf_op | source)
XLA Modules:
  0.0 104.4 jit_solution(12432908478963585017)
XLA Ops:
  0.7 0.0 copy-start
  0.7 1.1 %copy-done = bf16[2,44,3840]{2,0,1:T(2,128)(2,1)S(1)} copy-done((bf16[2,44,3840]{2,0,1:T(2,128)(2,1)S(1)}, bf16[2,44,3840]{2,0,1:T(2,128)(2,1)}, u32[]{:S(2)}) %copy-start) | copy-done | bytes 675864
  1.7 0.0 copy-start.1
  1.7 0.7 copy-done.1
  2.4 100.7 %shard_map.46 = bf16[6,1280,128]{2,1,0:T(8,128)(2,1)S(1)} custom-call(bf16[44,2,3840]{2,1,0:T(2,128)(2,1)S(1)} %bitcast.1, s32[40]{0:T(128)S(1)} %copy-done.1, s32[1]{0:T(128)S(6)} %copy.6.rows_ref, bf16[40,704,128]{2,1,0:T(8,128)(2,1)} %legendre.1), custom_call_target="tpu_custom_call" | custom-call | flops 1384120320 | bytes 20000000 | tf_op jit(solution)/shard_map/pallas_call | solution.py:290
  103.1 1.3 %copy.7 = bf16[6,1280,128]{2,1,0:T(8,128)(2,1)} copy(bf16[6,1280,128]{2,1,0:T(8,128)(2,1)S(1)} %shard_map.46) | data formatting | bytes 3932160
Async XLA Ops:
  0.7 1.1 %copy-start = (bf16[2,44,3840]{2,0,1:T(2,128)(2,1)S(1)}, bf16[2,44,3840]{2,0,1:T(2,128)(2,1)}, u32[]{:S(2)}) copy-start(bf16[2,44,3840]{2,0,1:T(2,128)(2,1)} %param.4) | copy-start | bytes 2027524
  1.7 0.7 copy-start.1

commit v4 on v3

--- a/solution.py
+++ b/solution.py
@@ -21,9 +21,9 @@
 
 
 def kernel(
-    coeffs, wave_ref, rows_ref, legendre, out,
-    raw, other, held, leg, natural, turned, stage, esend, erecv, asend,
-    leg_sem, raw_sem, z_send, z_recv, x_send, x_recv, e_send, e_recv, a_send, a_recv, self_sem,
+    coeffs, wavenumber, band_rows, legendre, out,
+    wave_ref, rows_ref, raw, other, held, leg, natural, turned, stage, esend, erecv, asend,
+    leg_sem, raw_sem, small_sem, z_send, z_recv, x_send, x_recv, e_send, e_recv, a_send, a_recv, self_sem,
 ):
     s = lax.axis_index("mset")
     b = lax.axis_index("band")
@@ -58,9 +58,17 @@
 
     raw_copy = pltpu.make_async_copy(coeffs, raw, raw_sem)
     raw_copy.start()
+    small_copies = [
+        pltpu.make_async_copy(src, dst, small_sem.at[i])
+        for i, (src, dst) in enumerate(((wavenumber, wave_ref), (band_rows, rows_ref)))
+    ]
+    for copy in small_copies:
+        copy.start()
     for k in range(CHUNKS):
         leg_copy(k).start()
     raw_copy.wait()
+    for copy in small_copies:
+        copy.wait()
 
     def pack(k):
         both = []
@@ -283,16 +291,18 @@
 
 
 def shards(coeffs, legendre, wavenumber, band_rows):
-    smem = pl.BlockSpec(memory_space=pltpu.SMEM)
+    hbm = pl.BlockSpec(memory_space=pltpu.HBM)
     anywhere = pl.BlockSpec(memory_space=pl.ANY)
     dma = pltpu.SemaphoreType.DMA
     sums = (CHUNKS, PIECES, FIELDS // PIECES, SLOTS, 128)
     return pl.pallas_call(
         kernel,
         out_shape=jax.ShapeDtypeStruct((6, 16 * CHUNKS * SLOTS, 128), jnp.bfloat16),
-        in_specs=[anywhere, smem, smem, anywhere],
+        in_specs=[hbm, hbm, hbm, hbm],
         out_specs=anywhere,
         scratch_shapes=[
+            pltpu.SMEM(wavenumber.shape, jnp.int32),
+            pltpu.SMEM(band_rows.shape, jnp.int32),
             pltpu.VMEM((44, 2, coeffs.shape[2]), jnp.bfloat16),
             pltpu.VMEM((CHUNKS, BLOCK, QUAD * FIELDS), jnp.bfloat16),
             pltpu.VMEM((16, CHUNKS, BLOCK, QUAD * FIELDS), jnp.bfloat16),
@@ -305,6 +315,7 @@
             pltpu.VMEM((CHUNKS, FIELDS, SLOTS, 128), jnp.bfloat16),
             dma((CHUNKS,)),
             dma,
+            dma((2,)),
             dma((7, CHUNKS)),
             dma((7, CHUNKS)),
             dma((8, CHUNKS)),
@@ -321,7 +332,7 @@
         cost_estimate=pl.CostEstimate(
             flops=2 * 40 * ROWS * 96 * 256, bytes_accessed=20_000_000, transcendentals=0
         ),
-    )(jnp.swapaxes(coeffs, 0, 1), wavenumber, band_rows, legendre)
+    )(pltpu.with_memory_space_constraint(jnp.swapaxes(coeffs, 0, 1), pltpu.HBM), pltpu.with_memory_space_constraint(wavenumber, pltpu.HBM), band_rows, legendre)
 
 
 def solution(mesh):

time: 105 us -> 103 us (0.981)
  local copies, waits for them, and re-layouts: 3.02 us -> 1.27 us
    unnamed x5 -> x1, local copies, waits for them, and re-layouts: 3.02 us -> 1.27 us
where the time goes in v4:
time: 103 us; the launch traced here: 102 us
  Pallas kernels  100 us (97%)
  local copies, waits for them, and re-layouts  1.27 us (1%)
    pallas_call x1, Pallas kernels, shards(): pl.pallas_call(kernel, out_shape=jax.ShapeDtypeStruct((6, 16 * CHUNKS * S...  100 us

profile of v4, /device:TPU:1, one launch (start us, length us, event | category | flops | bytes accessed | tf_op | source)
XLA Modules:
  0.0 102.3 jit_solution(13251350800944040921)
XLA Ops:
  0.7 100.4 %shard_map.46 = bf16[6,1280,128]{2,1,0:T(8,128)(2,1)S(1)} custom-call(bf16[44,2,3840]{2,1,0:T(2,128)(2,1)} %bitcast.1, s32[40]{0:T(128)} %wavenumber.1, s32[1]{0:T(128)S(6)} %copy.6.band_rows, bf16[40,704,128]{2,1,0:T(8,128)(2,1)} %legendre.1), custom_call_target="tpu_custom_call" | custom-call | flops 1384120320 | bytes 20000000 | tf_op jit(solution)/shard_map/pallas_call | solution.py:298
  101.1 1.3 %copy.7 = bf16[6,1280,128]{2,1,0:T(8,128)(2,1)} copy(bf16[6,1280,128]{2,1,0:T(8,128)(2,1)S(1)} %shard_map.46) | data formatting | bytes 3932160

commit v5 on v4

--- a/solution.py
+++ b/solution.py
@@ -266,7 +266,7 @@
             pack(i + 1)
             direct(i + 1)
 
-        for delay, stage_of in ((0, forward), (1, last), (2, transform), (3, drain), (3, combine)):
+        for delay, stage_of in ((0, forward), (1, last), (2, transform), (4, drain), (4, combine)):
             k = i - delay
 
             @pl.when((k >= 0) & (k < CHUNKS))
@@ -275,7 +275,7 @@
 
         return carry
 
-    lax.fori_loop(0, CHUNKS + 3, step, 0)
+    lax.fori_loop(0, CHUNKS + 4, step, 0)
 
     def finish(k, carry):
         for j in range(PIECES):

time: 103 us -> 103 us (level)
  no operation moved by 1% of the time
where the time goes in v5:
time: 103 us; the launch traced here: 102 us
  Pallas kernels  100 us (97%)
  local copies, waits for them, and re-layouts  1.27 us (1%)
    pallas_call x1, Pallas kernels, shards(): pl.pallas_call(kernel, out_shape=jax.ShapeDtypeStruct((6, 16 * CHUNKS * S...  100 us

profile of v5, /device:TPU:1, one launch (start us, length us, event | category | flops | bytes accessed | tf_op | source)
XLA Modules:
  0.0 102.3 jit_solution(7211603488732548745)
XLA Ops:
  0.7 100.3 %shard_map.46 = bf16[6,1280,128]{2,1,0:T(8,128)(2,1)S(1)} custom-call(bf16[44,2,3840]{2,1,0:T(2,128)(2,1)} %bitcast.1, s32[40]{0:T(128)} %wavenumber.1, s32[1]{0:T(128)S(6)} %copy.6.band_rows, bf16[40,704,128]{2,1,0:T(8,128)(2,1)} %legendre.1), custom_call_target="tpu_custom_call" | custom-call | flops 1384120320 | bytes 20000000 | tf_op jit(solution)/shard_map/pallas_call | solution.py:298
  101.0 1.3 %copy.7 = bf16[6,1280,128]{2,1,0:T(8,128)(2,1)} copy(bf16[6,1280,128]{2,1,0:T(8,128)(2,1)S(1)} %shard_map.46) | data formatting | bytes 3932160

commit v6 on v5

--- a/solution.py
+++ b/solution.py
@@ -261,12 +261,16 @@
             x_copy(j, k).wait_send()
 
     def step(i, carry):
+        @pl.when(i < CHUNKS)
+        def _():
+            forward(i)
+
         @pl.when(i + 1 < CHUNKS)
         def _():
             pack(i + 1)
             direct(i + 1)
 
-        for delay, stage_of in ((0, forward), (1, last), (2, transform), (4, drain), (4, combine)):
+        for delay, stage_of in ((1, last), (2, transform), (4, drain), (4, combine)):
             k = i - delay
 
             @pl.when((k >= 0) & (k < CHUNKS))

time: 103 us -> 109 us (1.058)
  Pallas kernels: 100 us -> 107 us
    pallas_call x1, Pallas kernels: 100 us -> 107 us  [shards(): pl.pallas_call(kernel, out_shape=jax.ShapeDtypeStruct((6, 16 * CHUNKS * S...]
where the time goes in v6:
time: 109 us
  Pallas kernels  107 us (98%)
  local copies, waits for them, and re-layouts  1.27 us (1%)
    pallas_call x1, Pallas kernels, shards(): pl.pallas_call(kernel, out_shape=jax.ShapeDtypeStruct((6, 16 * CHUNKS * S...  107 us

profile of v6, /device:TPU:1, one launch (start us, length us, event | category | flops | bytes accessed | tf_op | source)
XLA Modules:
  0.0 108.7 jit_solution(11455842566795445976)
XLA Ops:
  0.7 106.8 %shard_map.46 = bf16[6,1280,128]{2,1,0:T(8,128)(2,1)S(1)} custom-call(bf16[44,2,3840]{2,1,0:T(2,128)(2,1)} %bitcast.1, s32[40]{0:T(128)} %wavenumber.1, s32[1]{0:T(128)S(6)} %copy.6.band_rows, bf16[40,704,128]{2,1,0:T(8,128)(2,1)} %legendre.1), custom_call_target="tpu_custom_call" | custom-call | flops 1384120320 | bytes 20000000 | tf_op jit(solution)/shard_map/pallas_call | solution.py:302
  107.4 1.3 %copy.7 = bf16[6,1280,128]{2,1,0:T(8,128)(2,1)} copy(bf16[6,1280,128]{2,1,0:T(8,128)(2,1)S(1)} %shard_map.46) | data formatting | bytes 3932160
